TPU v7x, 256 devices: a whole 4x4x8 slice. The times are simulated.
256 devices in a mesh: lon: 64 (over x, z, core), lat: 4 (over y).
Axes of the slice: x: 4, y: 4, z: 8, core: 2. Of those that a mesh axis runs over, the one named last changes fastest.
Arguments:
- guidance: float32 [256, 32768], P('lat', 'lon'), may hold values from -36 to 36, as said below
- cond_lon: float32 [256, 32768], P('lat', 'lon'), may hold values from 0.2 to 5
- cond_lat: float32 [256, 32768], P('lat', 'lon'), may hold values from 0.2 to 5
Outputs:
- solution: float32 [256, 32768], P('lat', 'lon')
- residual: float32 [256, 32768], P('lat', 'lon')
Inputs may be any that keep to these rules, and one draw needn't show every extreme that they name: `guidance`: each entry is a product of a random value, a factor of its row and a factor of its column.
All inputs are finite; a program needn't handle non-finite values.
Results may differ from a plain program's by a relative error of at most 0.0003.
Values sent between devices are 32-bit elements; how exact they have to be, the bound alone decides.
A program may use at most 128 MiB of HBM per device.

v0:
```python
import jax
import jax.numpy as jnp
from jax import lax
from jax.experimental import pallas as pl
from jax.experimental.pallas import tpu as pltpu
from jax.sharding import PartitionSpec as P

OMEGA = 0.8
COARSE_SWEEPS = 8
NLAT, NLON, BLOCK = 4, 64, 16
ROWS, COLS = 64, 512
H = 16
PAD = 8
PAD2 = 16
N0 = ROWS + 2 * H
WIDE = COLS + 128
ALL = range(5)
MID = range(1, 4)
MESH = pl.DeviceIdType.MESH
F32 = jnp.float32

HALO = ((0, 1), (0, -1), (1, 0), (-1, 0), (1, 1), (1, -1), (-1, 1), (-1, -1))
SPREAD_LAT = (1, 2, 3)
SPREAD_LON = (1, -1, 2, -2)


def lanes(shape):
    return lax.broadcasted_iota(jnp.int32, shape, len(shape) - 1)


def rows_of(shape):
    return lax.broadcasted_iota(jnp.int32, shape, 0)


def roll_l(x, by):
    return pltpu.roll(x, by % x.shape[1], 1)


def ld(ref, start, n, blocks=ALL, stride=None):
    rows = pl.ds(start, n) if stride is None else pl.ds(start, n, stride=stride)
    return jnp.concatenate([ref[j, rows, :] for j in blocks], axis=1)


def st(ref, start, x, blocks=ALL, stride=None):
    n = x.shape[0]
    rows = pl.ds(start, n) if stride is None else pl.ds(start, n, stride=stride)
    for i, j in enumerate(blocks):
        ref[j, rows, :] = x[:, 128 * i:128 * (i + 1)]


def loop(r0, count, ch, body):
    if count == ch:
        body(r0)
    else:

        def step(k, carry):
            body(pl.multiple_of(r0 + k * ch, 8))
            return carry

        lax.fori_loop(0, count // ch, step, 0)


class Level:
    def __init__(self, s, pad, n, f, e, so, west, ae, aw, as_, an, w, wf, v, v2, q, r=None):
        self.s, self.pad, self.n = s, pad, n
        self.f, self.e, self.so, self.west = f, e, so, west
        self.ae, self.aw, self.as_, self.an, self.w, self.wf = ae, aw, as_, an, w, wf
        self.v, self.v2, self.q, self.r = v, v2, q, v2 if r is None else r


def coeffs(l, ch, keep=None, source=False):
    def body(r):
        p = l.pad + r
        e, so, no = ld(l.e, p, ch), ld(l.so, p, ch), ld(l.so, p - 1, ch)
        we = roll_l(e, l.s)
        wk = OMEGA / (((e + we) + so) + no)
        if keep is not None:
            row = rows_of(wk.shape) + r
            wk = jnp.where((row >= keep[0]) & (row < keep[1]), wk, 0.0)
        st(l.west, p, we)
        st(l.ae, p, wk * e)
        st(l.aw, p, wk * we)
        st(l.as_, p, wk * so)
        st(l.an, p, wk * no)
        if source:
            st(l.wf, p, wk * ld(l.f, p, ch))
        else:
            st(l.w, p, wk)

    loop(0, l.n, ch, body)


def sweep(l, src, dst, source, r0, count, ch, blocks=ALL):
    def body(r):
        p = l.pad + r
        v = ld(src, p, ch, blocks)
        x = ld(l.ae, p, ch, blocks) * roll_l(v, -l.s) + ld(l.aw, p, ch, blocks) * roll_l(v, l.s)
        y = ld(l.as_, p, ch, blocks) * ld(src, p + 1, ch, blocks) + ld(l.an, p, ch, blocks) * ld(src, p - 1, ch, blocks)
        z = (1.0 - OMEGA) * v
        if source:
            z = z + ld(l.wf, p, ch, blocks)
        st(dst, p, (y + z) + x, blocks)

    loop(r0, count, ch, body)


def operator(l, v, p, ch):
    x = ld(v, p, ch)
    lon = ld(l.e, p, ch) * (x - roll_l(x, -l.s)) + ld(l.west, p, ch) * (x - roll_l(x, l.s))
    lat = ld(l.so, p, ch) * (x - ld(v, p + 1, ch)) + ld(l.so, p - 1, ch) * (x - ld(v, p - 1, ch))
    return x, lat + lon


def remainder(l, ch):
    def body(r):
        p = l.pad + r
        st(l.r, p, ld(l.f, p, ch) - operator(l, l.v, p, ch)[1])

    loop(0, l.n, ch, body)


def pair(ref, start, n, odd, blocks=ALL):
    return ld(ref, start + odd, n, blocks, 2)


def restrict(l, c):
    ch = min(16, c.n)

    def body(a):
        x = pair(l.r, l.pad + 2 * a, ch, 0) + pair(l.r, l.pad + 2 * a, ch, 1)
        x = x + roll_l(x, -l.s)
        st(c.f, c.pad + a, x)
        st(c.wf, c.pad + a, x * ld(c.w, c.pad + a, ch))

    loop(0, c.n, ch, body)


def coarsen(l, c):
    ch = min(16, c.n)

    def body(a):
        x = pair(l.e, l.pad + 2 * a, ch, 0) + pair(l.e, l.pad + 2 * a, ch, 1)
        st(c.e, c.pad + a, roll_l(x, -l.s))
        y = pair(l.so, l.pad + 2 * a, ch, 1)
        st(c.so, c.pad + a, y + roll_l(y, -l.s))

    loop(0, c.n, ch, body)


def spread_rows(v, start, e, add, blocks=ALL):
    for odd in (0, 1):
        x = e
        if add:
            x = x + ld(v, start + odd, e.shape[0], blocks, 2)
        st(v, start + odd, x, blocks, 2)


def prolong(c, l, src, dst, a0, n, add, blocks=ALL):
    def body(a):
        e = ld(src, c.pad + a0 + a, 8, blocks)
        e = jnp.where((lanes(e.shape) & l.s) == 0, e, roll_l(e, l.s))
        spread_rows(dst, l.pad + 2 * (a0 + a), e, add, blocks)

    loop(0, n, 8, body)


def pick(x, index):
    return jnp.take_along_axis(x, index, axis=1, mode="promise_in_bounds")


def compact(x, offset):
    l = lanes((8, 128))
    index = (l % 32) * 4 + offset
    out = pick(x[:, 384:512], index)
    for j in (2, 1, 0):
        out = jnp.where(l < 32 * (j + 1), pick(x[:, 128 * j:128 * (j + 1)], index), out)
    return out


def expand(x, base):
    l = lanes((8, 128))
    q = l // 4
    own = x[2, pl.ds(base, 8), :]
    parts = [pick(own, q + 32 * j) for j in range(4)]
    east = pick(x[3, pl.ds(base, 8), :], q)
    west = pick(x[1, pl.ds(base, 8), :], q + 96)
    return jnp.concatenate(parts + [jnp.where(l < 64, east, west)], axis=1)


def kernel(
    b_in, e_in, s_in, sol, res,
    g, pk, re_, rw_, a0, ag, c, t1, got1, t2, got2,
    *rest,
):
    fine0, fine1, fine2, fine3, fine4, fine5 = rest[:9], rest[9:22], rest[22:32], rest[32:45], rest[45:58], rest[58:72]
    in_sem, a_send, a_recv, cs_send, cs_recv, fs_send, fs_recv, c1_send, c1_recv, c2_send, c2_recv = rest[72:]

    l0 = Level(1, PAD, N0, g.at[0], g.at[1], g.at[2], *fine0[:5], None, *fine0[5:])
    l1 = Level(2, PAD, N0 // 2, *fine1)
    l2 = Level(1, PAD2, 64, c.at[0], c.at[1], c.at[2], *fine2)
    l3 = Level(2, PAD, 32, *fine3)
    l4 = Level(4, PAD, 16, *fine4)
    l5 = Level(8, PAD, 8, *fine5)
    lat, lon = lax.axis_index("lat"), lax.axis_index("lon")

    def device(dlon, dlat):
        return {"lon": lax.rem(lon + dlon + NLON, NLON), "lat": lax.rem(lat + dlat + NLAT, NLAT)}

    block = (lon // BLOCK) * BLOCK
    inner = lax.rem(lon, BLOCK)

    def mate1(d):
        return {"lon": block + lax.rem(inner + d, BLOCK), "lat": lat}

    def mate2(d):
        return device(BLOCK * (d // 4), d % 4)

    top = PAD + H
    loads = [
        pltpu.make_async_copy(x.at[:, pl.ds(128 * j, 128)], g.at[i, j, pl.ds(top, ROWS)], in_sem.at[i, j])
        for i, x in enumerate((b_in, e_in, s_in))
        for j in range(4)
    ]
    barrier = pltpu.get_barrier_semaphore()
    greeted = [device(*d) for d in HALO] + [device(0, 2), device(2, 0), device(-2, 0)]
    greeted += [mate1(d) for d in range(1, BLOCK)] + [mate2(d) for d in range(4, 16)]
    for k, other in enumerate(greeted):
        pl.semaphore_signal(barrier, inc=1, device_id=other, device_id_type=MESH)
        if k == len(HALO) - 1:
            for copy in loads:
                copy.start()

    def clear(ref, l):
        zero = jnp.zeros((l.pad, WIDE), F32)
        st(ref, 0, zero)
        st(ref, l.pad + l.n, zero)

    for l in (l0, l1):
        for ref in (l.wf, l.v, l.v2, l.q):
            clear(ref, l)
    for l in (l2, l3, l4, l5):
        for ref in (l.wf, l.v, l.v2, l.q, l.so):
            clear(ref, l)
    for ref in (l2.ae, l2.aw, l2.as_, l2.an):
        clear(ref, l2)
    for ref in (l5.e, l5.r):
        clear(ref, l5)

    for copy in loads:
        copy.wait()

    l8 = lanes((8, 128))
    def pack(a):
        rows = pl.ds(pl.multiple_of(top + a, 8), 8)
        first = [g[i, 0, rows] for i in range(3)]
        last = [g[i, 3, rows] for i in range(3)]
        x = jnp.where(l8 < 16, first[0], jnp.where(l8 < 32, roll_l(first[1], 16), roll_l(first[2], 32)))
        y = jnp.where(l8 >= 112, last[0], jnp.where(l8 >= 96, roll_l(last[1], -16), roll_l(last[2], -32)))
        pk[pl.ds(a, 8)] = jnp.where(l8 < 64, x, y)

    loop(0, ROWS, 8, pack)

    own_rows = pl.ds(pl.multiple_of(PAD2 + lat * 16, 16), 16)

    for a in range(0, 16, 8):
        x = ld(g.at[1], top + 4 * a, 8, range(4), 4)
        for j in (1, 2, 3):
            x = x + ld(g.at[1], top + 4 * a + j, 8, range(4), 4)
        y = ld(g.at[2], top + 4 * a + 3, 8, range(4), 4)
        y = y + roll_l(y, -1)
        y = y + roll_l(y, -2)
        rows = pl.ds(pl.multiple_of(PAD2 + lat * 16 + a, 8), 8)
        c[1, 2, rows, :] = compact(x, 3)
        c[2, 2, rows, :] = compact(y, 0)

    pl.semaphore_wait(barrier, len(greeted))

    def send(src, dst, s_sem, r_sem, k, to):
        copy = pltpu.make_async_remote_copy(
            src_ref=src, dst_ref=dst, send_sem=s_sem.at[k], recv_sem=r_sem.at[k], device_id=to, device_id_type=MESH
        )
        copy.start()
        return copy

    halos = []
    for k, (dlon, dlat) in enumerate(HALO):
        first_row, count = {0: (0, ROWS), 1: (ROWS - H, H), -1: (0, H)}[dlat]
        to = {0: H, 1: 0, -1: H + ROWS}[dlat]
        if dlon == 0:
            src = g.at[:, pl.ds(0, 4), pl.ds(top + first_row, count)]
            dst = g.at[:, pl.ds(0, 4), pl.ds(PAD + to, count)]
        else:
            src = pk.at[pl.ds(first_row, count)]
            dst = (rw_ if dlon == 1 else re_).at[pl.ds(to, count)]
        halos.append(send(src, dst, a_send, a_recv, k, device(dlon, dlat)))

    def spread_lat(index, s_sem, r_sem):
        part = c.at[index, 2, own_rows]
        return [send(part, part, s_sem, r_sem, k, device(0, d)) for k, d in enumerate(SPREAD_LAT)]

    def spread_lon(index, s_sem, r_sem):
        rows = pl.ds(PAD2, 64)
        return [
            send(c.at[index, 2, rows], c.at[index, 2 - d, rows], s_sem, r_sem, 3 + k, device(d, 0))
            for k, d in enumerate(SPREAD_LON)
        ]

    conds = spread_lat(pl.ds(1, 2), cs_send, cs_recv)

    for copy in halos:
        copy.wait_recv()
    for copy in conds:
        copy.wait_recv()
    conds_lon = spread_lon(pl.ds(1, 2), cs_send, cs_recv)

    has_north = jnp.where(lat > 0, 1.0, 0.0).astype(F32)
    used = (l8 < 16) | (l8 >= 112)

    def unpack(a):
        x = jnp.where(l8 < 64, re_[pl.ds(a, 8)], rw_[pl.ds(a, 8)])
        for i, other in ((0, 0.0), (1, 1.0), (2, 1.0)):
            y = x if i == 0 else jnp.where(l8 < 64, roll_l(x, -16 * i), roll_l(x, 16 * i))
            g[i, 4, pl.ds(pl.multiple_of(PAD + a, 8), 8), :] = jnp.where(used, y, other)

    loop(0, N0, 8, unpack)
    g[2, :, PAD:PAD + H] = g[2, :, PAD:PAD + H] * has_north

    def bounds(halo, own):
        return jnp.where(lat > 0, 0, halo), jnp.where(lat < NLAT - 1, 2 * halo + own, halo + own)

    coeffs(l0, 16, bounds(H, ROWS), True)
    sweep(l0, l0.wf, l0.v, True, 0, N0, 16)
    coarsen(l0, l1)
    remainder(l0, 16)
    coeffs(l1, 16, bounds(H // 2, ROWS // 2))
    restrict(l0, l1)
    sweep(l1, l1.wf, l1.v, True, 0, 48, 16)
    remainder(l1, 16)
    for a in range(0, 16, 8):
        x = ld(l1.r, PAD + 8 + 2 * a, 8, range(4), 2) + ld(l1.r, PAD + 9 + 2 * a, 8, range(4), 2)
        rows = pl.ds(pl.multiple_of(PAD2 + lat * 16 + a, 8), 8)
        c[0, 2, rows, :] = compact(x + roll_l(x, -2), 0)
    fields = spread_lat(0, fs_send, fs_recv)

    for copy in conds_lon:
        copy.wait_recv()
    coeffs(l2, 16)
    coarsen(l2, l3)
    coeffs(l3, 16)
    coarsen(l3, l4)
    coeffs(l4, 16)
    coarsen(l4, l5)
    coeffs(l5, 8)


    def twice(l, v, source, r0, count, ch, blocks=ALL):
        sweep(l, v, l.v2, source, r0, count, ch, blocks)
        sweep(l, l.v2, v, source, r0, count, ch, blocks)

    def rise_coarse(name, source):
        u = [getattr(l, name) for l in (l0, l1, l2, l3, l4, l5)]
        twice(l5, u[5], source, 0, 8, 8, MID)
        prolong(l5, l4, u[5], u[4], 0, 8, source, MID)
        twice(l4, u[4], source, 0, 16, 16, MID)
        prolong(l4, l3, u[4], u[3], 0, 16, source, MID)
        twice(l3, u[3], source, 0, 32, 16, MID)
        near = lat * 8 - 4
        prolong(l3, l2, u[3], u[2], near, 16, source, MID)
        near = pl.multiple_of(lat * 16 - 8, 8)
        twice(l2, u[2], source, near, 32, 16, MID)

    def rise_fine(name, source):
        u = [getattr(l, name) for l in (l0, l1, l2)]
        for i in range(3):
            e = expand(u[2], PAD2 + lat * 16 - 4 + 8 * i)
            spread_rows(u[1], PAD + 16 * i, e, source)
        twice(l1, u[1], source, 0, 48, 16)
        prolong(l1, l0, u[1], u[0], 0, 48, source)
        twice(l0, u[0], source, 8, 80, 16)

    def applied(v, out, sums, n):
        def body(k, carry):
            r = pl.multiple_of(k * 16, 16)
            x, av = operator(l0, v, top + r, 16)
            x, av = x[:, :COLS], av[:, :COLS]
            out[pl.ds(r, 16)] = av
            more = sums(pl.ds(r, 16), ld(l0.f, top + r, 16, range(4)), x, av)
            return tuple(y + (z[:8] + z[8:]) for y, z in zip(carry, more))

        return lax.fori_loop(0, ROWS // 16, body, (jnp.zeros((8, COLS), F32),) * n)

    st(l5.q, PAD, jnp.ones((8, WIDE), F32))
    rise_coarse("q", False)
    for copy in halos + conds:
        copy.wait_send()
    for copy in fields:
        copy.wait_recv()
    fields_lon = spread_lon(0, fs_send, fs_recv)
    rise_fine("q", False)
    for copy in fields + conds_lon:
        copy.wait_send()
    sums_q = applied(l0.q, ag, lambda rows, b, v, av: (b * v, v * av), 2)

    for copy in fields_lon:
        copy.wait_recv()

    def first(r):
        st(l2.wf, PAD2 + r, ld(l2.w, PAD2 + r, 16) * ld(l2.f, PAD2 + r, 16))

    loop(0, 64, 16, first)
    sweep(l2, l2.wf, l2.v, True, 0, 64, 16)
    remainder(l2, 16)
    for l, coarse in ((l2, l3), (l3, l4), (l4, l5)):
        restrict(l, coarse)
        sweep(coarse, coarse.wf, coarse.v, True, 0, coarse.n, min(16, coarse.n))
        remainder(coarse, min(16, coarse.n))

    x = pair(l5.r, PAD, 8, 0) + pair(l5.r, PAD, 8, 1)
    f6 = x + roll_l(x, -8)
    x = pair(l5.e, PAD, 8, 0) + pair(l5.e, PAD, 8, 1)
    e6 = roll_l(x, -8)
    x = pair(l5.so, PAD, 8, 1)
    s6 = x + roll_l(x, -8)
    row6, lane6 = rows_of((8, WIDE)), lanes((8, WIDE))
    west6 = roll_l(e6, 16)
    north6 = jnp.where(row6 == 0, 0.0, pltpu.roll(s6, 1, 0))
    w6 = jnp.where(row6 < 4, OMEGA / (((e6 + west6) + s6) + north6), 0.0)
    ae6, aw6, as6, an6, wf6 = w6 * e6, w6 * west6, w6 * s6, w6 * north6, w6 * f6
    field = wf6
    for _ in range(COARSE_SWEEPS - 1):
        x = ae6 * roll_l(field, -16) + aw6 * roll_l(field, 16)
        y = as6 * pltpu.roll(field, 7, 0) + an6 * pltpu.roll(field, 1, 0)
        field = (((1.0 - OMEGA) * field + wf6) + y) + x
    lon6 = e6 * (field - roll_l(field, -16)) + west6 * (field - roll_l(field, 16))
    lat6 = s6 * (field - pltpu.roll(field, 7, 0)) + north6 * (field - pltpu.roll(field, 1, 0))
    left = f6 - (lon6 + lat6)
    mine = ((lane6 & 15) == 0) & (lane6 >= 256) & (lane6 < 384)
    left = jnp.where(mine & (row6 == lat), left, 0.0)[:, 256:384]
    last = jnp.where(mine & (row6 == 3) & (lat == 3), s6, 0.0)[:, 256:384]

    e = jnp.where((lane6 & 8) == 0, field, roll_l(field, 8))
    for odd in (0, 1):
        st(l5.r, odd, e, ALL, 2)
    st(l5.v, PAD, ld(l5.v, PAD, 8) + ld(l5.r, 0, 8))
    rise_coarse("v", True)
    rise_fine("v", True)
    sums_v = applied(l0.v, a0, lambda rows, b, v, av: (b * v, v * av, v * ag[rows]), 3)

    def wait_all(got, sem):
        pltpu.make_async_copy(got, got, sem.at[0]).wait()

    def fold(x):
        return (x[:, 0:128] + x[:, 128:256]) + (x[:, 256:384] + x[:, 384:512])

    seven = [left, last, fold(sums_v[0]), fold(sums_q[0]), fold(sums_v[1]), fold(sums_v[2]), fold(sums_q[1])]
    row = rows_of((8, 128))
    total = jnp.zeros((8, 128), F32)
    for i, x in enumerate(seven):
        total = jnp.where(row == i, jnp.sum(x, axis=0, keepdims=True), total)
    t1[...] = total
    for d in range(1, 16):
        send(t1, got1.at[d - 1], c1_send, c1_recv, 0, mate1(d))
    for copy in fields_lon:
        copy.wait_send()
    wait_all(got1, c1_recv)

    def gathered(total, got):
        parts = [total] + [got[d] for d in range(15)]
        while len(parts) > 1:
            parts = [x + y for x, y in zip(parts[::2], parts[1::2])]
        return parts[0]

    total = gathered(total, got1)
    t2[...] = total
    for d in range(1, 16):
        send(t2, got2.at[d - 1], c2_send, c2_recv, 0, mate2(d))
    wait_all(got1, c1_send)
    wait_all(got2, c2_recv)
    total = gathered(total, got2)
    for by in (64, 32, 16, 8, 4, 2, 1):
        total = total + pltpu.roll(total, by, 1)
    n_left, n_last, bv, bq, vav, vaq, qaq = [total[i:i + 1] for i in range(7)]
    const = n_left / n_last
    step = (bv + const * bq) / ((vav + (2.0 * const) * vaq) + (const * const) * qaq)
    both = jnp.concatenate([step * const] * 4, axis=1)
    step = jnp.concatenate([step] * 4, axis=1)

    def final(k, carry):
        r = pl.multiple_of(k * 16, 16)
        rows = pl.ds(r, 16)
        sol[rows] = step * ld(l0.v, top + r, 16, range(4)) + both * ld(l0.q, top + r, 16, range(4))
        res[rows] = ld(l0.f, top + r, 16, range(4)) - (step * a0[rows] + both * ag[rows])
        return carry

    lax.fori_loop(0, 4, final, 0)
    wait_all(got2, c2_send)


def body(guidance, cond_lon, cond_lat):
    def vm(*shape):
        return pltpu.VMEM(shape, F32)

    def wide(n, count):
        return [vm(5, n, 128)] * count

    dma = pltpu.SemaphoreType.DMA
    scratch = [vm(3, 5, N0 + 2 * PAD, 128), vm(ROWS, 128), vm(N0, 128), vm(N0, 128), vm(ROWS, COLS), vm(ROWS, COLS)]
    scratch += [vm(3, 5, 64 + 2 * PAD2, 128), vm(8, 128), vm(15, 8, 128), vm(8, 128), vm(15, 8, 128)]
    scratch += wide(N0 + 2 * PAD, 9) + wide(N0 // 2 + 2 * PAD, 13) + wide(64 + 2 * PAD2, 10)
    scratch += wide(32 + 2 * PAD, 13) + wide(16 + 2 * PAD, 13) + wide(8 + 2 * PAD, 14)
    scratch += [dma((3, 4)), dma((8,)), dma((8,)), dma((7,)), dma((7,)), dma((7,)), dma((7,))] + [dma((1,))] * 4
    return pl.pallas_call(
        kernel,
        out_shape=(jax.ShapeDtypeStruct((ROWS, COLS), F32),) * 2,
        in_specs=[pl.BlockSpec(memory_space=pltpu.HBM)] * 3,
        out_specs=(pl.BlockSpec(memory_space=pltpu.VMEM),) * 2,
        scratch_shapes=scratch,
        compiler_params=pltpu.CompilerParams(
            collective_id=0, has_side_effects=True, vmem_limit_bytes=63 * 1024 * 1024
        ),
        cost_estimate=pl.CostEstimate(flops=10_000_000, bytes_accessed=655360, transcendentals=0),
    )(guidance, cond_lon, cond_lat)


def solution(mesh):
    spec = P("lat", "lon")
    return jax.shard_map(body, mesh=mesh, in_specs=(spec,) * 3, out_specs=(spec,) * 2, check_vma=False)
```

profile of v0, /device:TPU:1, one launch (start us, length us, event | category | flops | bytes accessed | tf_op | source)
XLA Modules:
  0.0 48.5 jit_solution(11646408356409851826)
XLA Ops:
  0.6 45.5 %shard_map.50 = (f32[64,512]{1,0:T(8,128)}, f32[64,512]{1,0:T(8,128)}) custom-call(f32[64,512]{1,0:T(8,128)} %b_in.1, f32[64,512]{1,0:T(8,128)} %e_in.1, f32[64,512]{1,0:T(8,128)} %s_in.1), custom_call_target="tpu_custom_call" | custom-call | flops 10000000 | bytes 655360 | tf_op jit(solution)/shard_map/pallas_call | solution.py:512
  46.2 0.0 copy-start
  46.2 1.6 %copy.7 = f32[64,512]{1,0:T(8,128)} copy(f32[64,512]{1,0:T(8,128)} %get-tuple-element.4) | data formatting | bytes 262144
  47.8 0.0 copy-done
  47.8 0.7 %copy.8 = f32[64,512]{1,0:T(8,128)} copy(f32[64,512]{1,0:T(8,128)S(1)} %copy-done) | data formatting | bytes 262144
Async XLA Ops:
  46.2 1.6 %copy-start = (f32[64,512]{1,0:T(8,128)S(1)}, f32[64,512]{1,0:T(8,128)}, u32[]{:S(2)}) copy-start(f32[64,512]{1,0:T(8,128)} %get-tuple-element.5) | copy-start | bytes 393220
where the time goes:
time: 48.6 us; the launch traced here: 48.5 us
  Pallas kernels  45.5 us (94%)
  local copies, waits for them, and re-layouts  2.26 us (5%)
  between operations  0.65 us (1%)
    pallas_call x1, Pallas kernels, body(): pl.pallas_call(kernel, out_shape=(jax.ShapeDtypeStruct((ROWS, COLS), F32)...  45.5 us
    unnamed x4, local copies, waits for them, and re-layouts  2.26 us

commit v1 on v0

--- a/solution.py
+++ b/solution.py
@@ -49,15 +49,8 @@
 
 
 def loop(r0, count, ch, body):
-    if count == ch:
-        body(r0)
-    else:
-
-        def step(k, carry):
-            body(pl.multiple_of(r0 + k * ch, 8))
-            return carry
-
-        lax.fori_loop(0, count // ch, step, 0)
+    for k in range(count // ch):
+        body(r0 + k * ch)
 
 
 class Level:
@@ -132,19 +125,17 @@
         st(c.f, c.pad + a, x)
         st(c.wf, c.pad + a, x * ld(c.w, c.pad + a, ch))
 
-    loop(0, c.n, ch, body)
+    for a in range(0, c.n, ch):
+        body(a)
 
 
 def coarsen(l, c):
     ch = min(16, c.n)
-
-    def body(a):
+    for a in range(0, c.n, ch):
         x = pair(l.e, l.pad + 2 * a, ch, 0) + pair(l.e, l.pad + 2 * a, ch, 1)
         st(c.e, c.pad + a, roll_l(x, -l.s))
         y = pair(l.so, l.pad + 2 * a, ch, 1)
         st(c.so, c.pad + a, y + roll_l(y, -l.s))
-
-    loop(0, c.n, ch, body)
 
 
 def spread_rows(v, start, e, add, blocks=ALL):
@@ -156,12 +147,10 @@
 
 
 def prolong(c, l, src, dst, a0, n, add, blocks=ALL):
-    def body(a):
+    for a in range(0, n, 8):
         e = ld(src, c.pad + a0 + a, 8, blocks)
         e = jnp.where((lanes(e.shape) & l.s) == 0, e, roll_l(e, l.s))
         spread_rows(dst, l.pad + 2 * (a0 + a), e, add, blocks)
-
-    loop(0, n, 8, body)
 
 
 def pick(x, index):
@@ -250,15 +239,13 @@
         copy.wait()
 
     l8 = lanes((8, 128))
-    def pack(a):
-        rows = pl.ds(pl.multiple_of(top + a, 8), 8)
+    for k in range(ROWS // 8):
+        rows = slice(top + 8 * k, top + 8 * k + 8)
         first = [g[i, 0, rows] for i in range(3)]
         last = [g[i, 3, rows] for i in range(3)]
         x = jnp.where(l8 < 16, first[0], jnp.where(l8 < 32, roll_l(first[1], 16), roll_l(first[2], 32)))
         y = jnp.where(l8 >= 112, last[0], jnp.where(l8 >= 96, roll_l(last[1], -16), roll_l(last[2], -32)))
-        pk[pl.ds(a, 8)] = jnp.where(l8 < 64, x, y)
-
-    loop(0, ROWS, 8, pack)
+        pk[8 * k:8 * k + 8] = jnp.where(l8 < 64, x, y)
 
     own_rows = pl.ds(pl.multiple_of(PAD2 + lat * 16, 16), 16)
 
@@ -315,14 +302,11 @@
 
     has_north = jnp.where(lat > 0, 1.0, 0.0).astype(F32)
     used = (l8 < 16) | (l8 >= 112)
-
-    def unpack(a):
-        x = jnp.where(l8 < 64, re_[pl.ds(a, 8)], rw_[pl.ds(a, 8)])
+    for k in range(N0 // 8):
+        x = jnp.where(l8 < 64, re_[8 * k:8 * k + 8], rw_[8 * k:8 * k + 8])
         for i, other in ((0, 0.0), (1, 1.0), (2, 1.0)):
             y = x if i == 0 else jnp.where(l8 < 64, roll_l(x, -16 * i), roll_l(x, 16 * i))
-            g[i, 4, pl.ds(pl.multiple_of(PAD + a, 8), 8), :] = jnp.where(used, y, other)
-
-    loop(0, N0, 8, unpack)
+            g[i, 4, PAD + 8 * k:PAD + 8 * k + 8, :] = jnp.where(used, y, other)
     g[2, :, PAD:PAD + H] = g[2, :, PAD:PAD + H] * has_north
 
     def bounds(halo, own):
@@ -379,15 +363,17 @@
         twice(l0, u[0], source, 8, 80, 16)
 
     def applied(v, out, sums, n):
-        def body(k, carry):
-            r = pl.multiple_of(k * 16, 16)
+        def body(r, carry):
             x, av = operator(l0, v, top + r, 16)
             x, av = x[:, :COLS], av[:, :COLS]
             out[pl.ds(r, 16)] = av
             more = sums(pl.ds(r, 16), ld(l0.f, top + r, 16, range(4)), x, av)
             return tuple(y + (z[:8] + z[8:]) for y, z in zip(carry, more))
 
-        return lax.fori_loop(0, ROWS // 16, body, (jnp.zeros((8, COLS), F32),) * n)
+        carry = (jnp.zeros((8, COLS), F32),) * n
+        for r in range(0, ROWS, 16):
+            carry = body(r, carry)
+        return carry
 
     st(l5.q, PAD, jnp.ones((8, WIDE), F32))
     rise_coarse("q", False)
@@ -485,14 +471,10 @@
     both = jnp.concatenate([step * const] * 4, axis=1)
     step = jnp.concatenate([step] * 4, axis=1)
 
-    def final(k, carry):
-        r = pl.multiple_of(k * 16, 16)
+    for r in range(0, ROWS, 16):
         rows = pl.ds(r, 16)
         sol[rows] = step * ld(l0.v, top + r, 16, range(4)) + both * ld(l0.q, top + r, 16, range(4))
         res[rows] = ld(l0.f, top + r, 16, range(4)) - (step * a0[rows] + both * ag[rows])
-        return carry
-
-    lax.fori_loop(0, 4, final, 0)
     wait_all(got2, c2_send)
 
 

time: 48.6 us -> 43.4 us (0.89)
  Pallas kernels: 45.5 us -> 40.3 us
    pallas_call x1, Pallas kernels: 45.5 us -> 40.3 us  [body(): pl.pallas_call(kernel, out_shape=(jax.ShapeDtypeStruct((ROWS, COLS), F32)...]
where the time goes in v1:
time: 43.4 us; the launch traced here: 43.2 us
  Pallas kernels  40.3 us (93%)
  local copies, waits for them, and re-layouts  2.26 us (5%)
  between operations  0.65 us (1%)
    pallas_call x1, Pallas kernels, body(): pl.pallas_call(kernel, out_shape=(jax.ShapeDtypeStruct((ROWS, COLS), F32)...  40.3 us
    unnamed x4, local copies, waits for them, and re-layouts  2.26 us

profile of v1, /device:TPU:1, one launch (start us, length us, event | category | flops | bytes accessed | tf_op | source)
XLA Modules:
  0.0 43.2 jit_solution(1359199919848100428)
XLA Ops:
  0.6 40.3 %shard_map.50 = (f32[64,512]{1,0:T(8,128)}, f32[64,512]{1,0:T(8,128)}) custom-call(f32[64,512]{1,0:T(8,128)} %b_in.1, f32[64,512]{1,0:T(8,128)} %e_in.1, f32[64,512]{1,0:T(8,128)} %s_in.1), custom_call_target="tpu_custom_call" | custom-call | flops 10000000 | bytes 655360 | tf_op jit(solution)/shard_map/pallas_call | solution.py:494
  40.9 0.0 copy-start
  40.9 1.6 %copy.7 = f32[64,512]{1,0:T(8,128)} copy(f32[64,512]{1,0:T(8,128)} %get-tuple-element.4) | data formatting | bytes 262144
  42.5 0.0 copy-done
  42.5 0.7 %copy.8 = f32[64,512]{1,0:T(8,128)} copy(f32[64,512]{1,0:T(8,128)S(1)} %copy-done) | data formatting | bytes 262144
Async XLA Ops:
  40.9 1.6 %copy-start = (f32[64,512]{1,0:T(8,128)S(1)}, f32[64,512]{1,0:T(8,128)}, u32[]{:S(2)}) copy-start(f32[64,512]{1,0:T(8,128)} %get-tuple-element.5) | copy-start | bytes 393220

commit v2 on v1

--- a/solution.py
+++ b/solution.py
@@ -19,7 +19,6 @@
 MESH = pl.DeviceIdType.MESH
 F32 = jnp.float32
 
-HALO = ((0, 1), (0, -1), (1, 0), (-1, 0), (1, 1), (1, -1), (-1, 1), (-1, -1))
 SPREAD_LAT = (1, 2, 3)
 SPREAD_LON = (1, -1, 2, -2)
 
@@ -182,7 +181,7 @@
     *rest,
 ):
     fine0, fine1, fine2, fine3, fine4, fine5 = rest[:9], rest[9:22], rest[22:32], rest[32:45], rest[45:58], rest[58:72]
-    in_sem, a_send, a_recv, cs_send, cs_recv, fs_send, fs_recv, c1_send, c1_recv, c2_send, c2_recv = rest[72:]
+    in_sem, a_send, a_recv, cs_send, cs_recv, fs_send, fs_recv, c1_send, c1_recv, c2_send, c2_recv, token = rest[72:]
 
     l0 = Level(1, PAD, N0, g.at[0], g.at[1], g.at[2], *fine0[:5], None, *fine0[5:])
     l1 = Level(2, PAD, N0 // 2, *fine1)
@@ -211,13 +210,20 @@
         for j in range(4)
     ]
     barrier = pltpu.get_barrier_semaphore()
-    greeted = [device(*d) for d in HALO] + [device(0, 2), device(2, 0), device(-2, 0)]
-    greeted += [mate1(d) for d in range(1, BLOCK)] + [mate2(d) for d in range(4, 16)]
-    for k, other in enumerate(greeted):
+    greeted = [device(*d) for d in ((1, 0), (-1, 0), (0, 1), (0, -1), (2, 0), (-2, 0), (0, 2))]
+    for other in greeted:
         pl.semaphore_signal(barrier, inc=1, device_id=other, device_id_type=MESH)
-        if k == len(HALO) - 1:
-            for copy in loads:
-                copy.start()
+    for copy in loads:
+        copy.start()
+
+    rounds = [[(2, 0), (-2, 0)], [(4, 0), (-4, 0)], [(8, 0), (-8, 0)], [(16, 0), (-16, 0)], [(0, 1), (0, 2), (0, 3)]]
+
+    def tell(k):
+        for d in rounds[k]:
+            pl.semaphore_signal(token.at[k], inc=1, device_id=device(*d), device_id_type=MESH)
+
+    def hear(k):
+        pl.semaphore_wait(token.at[k], len(rounds[k]))
 
     def clear(ref, l):
         zero = jnp.zeros((l.pad, WIDE), F32)
@@ -239,13 +245,16 @@
         copy.wait()
 
     l8 = lanes((8, 128))
-    for k in range(ROWS // 8):
-        rows = slice(top + 8 * k, top + 8 * k + 8)
+    def pack(k):
+        rows = slice(PAD + 8 * k, PAD + 8 * k + 8)
         first = [g[i, 0, rows] for i in range(3)]
         last = [g[i, 3, rows] for i in range(3)]
         x = jnp.where(l8 < 16, first[0], jnp.where(l8 < 32, roll_l(first[1], 16), roll_l(first[2], 32)))
         y = jnp.where(l8 >= 112, last[0], jnp.where(l8 >= 96, roll_l(last[1], -16), roll_l(last[2], -32)))
         pk[8 * k:8 * k + 8] = jnp.where(l8 < 64, x, y)
+
+    for k in range(H // 8, (H + ROWS) // 8):
+        pack(k)
 
     own_rows = pl.ds(pl.multiple_of(PAD2 + lat * 16, 16), 16)
 
@@ -269,17 +278,19 @@
         copy.start()
         return copy
 
-    halos = []
-    for k, (dlon, dlat) in enumerate(HALO):
-        first_row, count = {0: (0, ROWS), 1: (ROWS - H, H), -1: (0, H)}[dlat]
-        to = {0: H, 1: 0, -1: H + ROWS}[dlat]
-        if dlon == 0:
-            src = g.at[:, pl.ds(0, 4), pl.ds(top + first_row, count)]
-            dst = g.at[:, pl.ds(0, 4), pl.ds(PAD + to, count)]
-        else:
-            src = pk.at[pl.ds(first_row, count)]
-            dst = (rw_ if dlon == 1 else re_).at[pl.ds(to, count)]
-        halos.append(send(src, dst, a_send, a_recv, k, device(dlon, dlat)))
+    def rows_out(k, dlat, first, to):
+        src = g.at[:, pl.ds(0, 4), pl.ds(PAD + first, H)]
+        return send(src, g.at[:, pl.ds(0, 4), pl.ds(PAD + to, H)], a_send, a_recv, k, device(0, dlat))
+
+    def edges_out(k, first, n):
+        rows = pl.ds(first, n)
+        return [
+            send(pk.at[rows], rw_.at[rows], a_send, a_recv, k, device(1, 0)),
+            send(pk.at[rows], re_.at[rows], a_send, a_recv, k + 1, device(-1, 0)),
+        ]
+
+    halos = [rows_out(0, 1, ROWS, 0), rows_out(1, -1, H, H + ROWS)] + edges_out(2, H, ROWS)
+    tell(0)
 
     def spread_lat(index, s_sem, r_sem):
         part = c.at[index, 2, own_rows]
@@ -294,8 +305,15 @@
 
     conds = spread_lat(pl.ds(1, 2), cs_send, cs_recv)
 
-    for copy in halos:
+    for k, first in ((0, 0), (1, H + ROWS)):
+        halos[k].wait_recv()
+        for i in range(first // 8, (first + H) // 8):
+            pack(i)
+        halos += edges_out(4 + 2 * k, first, H)
+    for copy in halos[2:]:
         copy.wait_recv()
+    hear(0)
+    tell(1)
     for copy in conds:
         copy.wait_recv()
     conds_lon = spread_lon(pl.ds(1, 2), cs_send, cs_recv)
@@ -325,6 +343,8 @@
         rows = pl.ds(pl.multiple_of(PAD2 + lat * 16 + a, 8), 8)
         c[0, 2, rows, :] = compact(x + roll_l(x, -2), 0)
     fields = spread_lat(0, fs_send, fs_recv)
+    hear(1)
+    tell(2)
 
     for copy in conds_lon:
         copy.wait_recv()
@@ -382,6 +402,8 @@
     for copy in fields:
         copy.wait_recv()
     fields_lon = spread_lon(0, fs_send, fs_recv)
+    hear(2)
+    tell(3)
     rise_fine("q", False)
     for copy in fields + conds_lon:
         copy.wait_send()
@@ -389,6 +411,8 @@
 
     for copy in fields_lon:
         copy.wait_recv()
+    hear(3)
+    tell(4)
 
     def first(r):
         st(l2.wf, PAD2 + r, ld(l2.w, PAD2 + r, 16) * ld(l2.f, PAD2 + r, 16))
@@ -443,6 +467,7 @@
     total = jnp.zeros((8, 128), F32)
     for i, x in enumerate(seven):
         total = jnp.where(row == i, jnp.sum(x, axis=0, keepdims=True), total)
+    hear(4)
     t1[...] = total
     for d in range(1, 16):
         send(t1, got1.at[d - 1], c1_send, c1_recv, 0, mate1(d))
@@ -486,11 +511,11 @@
         return [vm(5, n, 128)] * count
 
     dma = pltpu.SemaphoreType.DMA
-    scratch = [vm(3, 5, N0 + 2 * PAD, 128), vm(ROWS, 128), vm(N0, 128), vm(N0, 128), vm(ROWS, COLS), vm(ROWS, COLS)]
+    scratch = [vm(3, 5, N0 + 2 * PAD, 128), vm(N0, 128), vm(N0, 128), vm(N0, 128), vm(ROWS, COLS), vm(ROWS, COLS)]
     scratch += [vm(3, 5, 64 + 2 * PAD2, 128), vm(8, 128), vm(15, 8, 128), vm(8, 128), vm(15, 8, 128)]
     scratch += wide(N0 + 2 * PAD, 9) + wide(N0 // 2 + 2 * PAD, 13) + wide(64 + 2 * PAD2, 10)
     scratch += wide(32 + 2 * PAD, 13) + wide(16 + 2 * PAD, 13) + wide(8 + 2 * PAD, 14)
-    scratch += [dma((3, 4)), dma((8,)), dma((8,)), dma((7,)), dma((7,)), dma((7,)), dma((7,))] + [dma((1,))] * 4
+    scratch += [dma((3, 4)), dma((8,)), dma((8,)), dma((7,)), dma((7,)), dma((7,)), dma((7,))] + [dma((1,))] * 4 + [pltpu.SemaphoreType.REGULAR((5,))]
     return pl.pallas_call(
         kernel,
         out_shape=(jax.ShapeDtypeStruct((ROWS, COLS), F32),) * 2,

time: 43.4 us -> 44.9 us (1.035)
  Pallas kernels: 40.3 us -> 41.8 us
    pallas_call x1, Pallas kernels: 40.3 us -> 41.8 us  [body(): pl.pallas_call(kernel, out_shape=(jax.ShapeDtypeStruct((ROWS, COLS), F32)...]
where the time goes in v2:
time: 44.9 us; the launch traced here: 44.7 us
  Pallas kernels  41.8 us (93%)
  local copies, waits for them, and re-layouts  2.26 us (5%)
  between operations  0.65 us (1%)
    pallas_call x1, Pallas kernels, body(): pl.pallas_call(kernel, out_shape=(jax.ShapeDtypeStruct((ROWS, COLS), F32)...  41.8 us
    unnamed x4, local copies, waits for them, and re-layouts  2.26 us

profile of v2, /device:TPU:1, one launch (start us, length us, event | category | flops | bytes accessed | tf_op | source)
XLA Modules:
  0.0 44.7 jit_solution(13833125947022780985)
XLA Ops:
  0.6 41.8 %shard_map.50 = (f32[64,512]{1,0:T(8,128)}, f32[64,512]{1,0:T(8,128)}) custom-call(f32[64,512]{1,0:T(8,128)} %b_in.1, f32[64,512]{1,0:T(8,128)} %e_in.1, f32[64,512]{1,0:T(8,128)} %s_in.1), custom_call_target="tpu_custom_call" | custom-call | flops 10000000 | bytes 655360 | tf_op jit(solution)/shard_map/pallas_call | solution.py:519
  42.5 0.0 copy-start
  42.5 1.6 %copy.7 = f32[64,512]{1,0:T(8,128)} copy(f32[64,512]{1,0:T(8,128)} %get-tuple-element.4) | data formatting | bytes 262144
  44.1 0.0 copy-done
  44.1 0.7 %copy.8 = f32[64,512]{1,0:T(8,128)} copy(f32[64,512]{1,0:T(8,128)S(1)} %copy-done) | data formatting | bytes 262144
Async XLA Ops:
  42.5 1.6 %copy-start = (f32[64,512]{1,0:T(8,128)S(1)}, f32[64,512]{1,0:T(8,128)}, u32[]{:S(2)}) copy-start(f32[64,512]{1,0:T(8,128)} %get-tuple-element.5) | copy-start | bytes 393220

commit v3 on v1

--- a/solution.py
+++ b/solution.py
@@ -19,9 +19,13 @@
 MESH = pl.DeviceIdType.MESH
 F32 = jnp.float32
 
-HALO = ((0, 1), (0, -1), (1, 0), (-1, 0), (1, 1), (1, -1), (-1, 1), (-1, -1))
+HALO = ((1, 1), (1, -1), (-1, 1), (-1, -1), (1, 0), (-1, 0), (0, 1), (0, -1))
 SPREAD_LAT = (1, 2, 3)
-SPREAD_LON = (1, -1, 2, -2)
+SPREAD_LON = (2, -2, 1, -1)
+SPREAD = ((2, 2), (-2, 2), (1, 2), (-1, 2), (2, 1), (2, -1), (-2, 1), (-2, -1), (0, 2), (2, 0), (-2, 0))
+SPREAD += ((1, 1), (1, -1), (-1, 1), (-1, -1), (0, 1), (0, -1), (1, 0), (-1, 0))
+FAR1 = (8, 7, 9, 6, 10, 5, 11, 4, 12, 3, 13, 2, 14, 1, 15)
+FAR2 = (10, 9, 11, 6, 14, 2, 8, 5, 7, 13, 15, 1, 3, 4, 12)
 
 
 def lanes(shape):
@@ -211,7 +215,7 @@
         for j in range(4)
     ]
     barrier = pltpu.get_barrier_semaphore()
-    greeted = [device(*d) for d in HALO] + [device(0, 2), device(2, 0), device(-2, 0)]
+    greeted = [device(*d) for d in HALO + SPREAD[:11]]
     greeted += [mate1(d) for d in range(1, BLOCK)] + [mate2(d) for d in range(4, 16)]
     for k, other in enumerate(greeted):
         pl.semaphore_signal(barrier, inc=1, device_id=other, device_id_type=MESH)
@@ -324,7 +328,10 @@
         x = ld(l1.r, PAD + 8 + 2 * a, 8, range(4), 2) + ld(l1.r, PAD + 9 + 2 * a, 8, range(4), 2)
         rows = pl.ds(pl.multiple_of(PAD2 + lat * 16 + a, 8), 8)
         c[0, 2, rows, :] = compact(x + roll_l(x, -2), 0)
-    fields = spread_lat(0, fs_send, fs_recv)
+    fields = [
+        send(c.at[0, 2, own_rows], c.at[0, 2 - d[0], own_rows], fs_send, fs_recv, k, device(*d))
+        for k, d in enumerate(SPREAD)
+    ]
 
     for copy in conds_lon:
         copy.wait_recv()
@@ -379,15 +386,12 @@
     rise_coarse("q", False)
     for copy in halos + conds:
         copy.wait_send()
-    for copy in fields:
-        copy.wait_recv()
-    fields_lon = spread_lon(0, fs_send, fs_recv)
     rise_fine("q", False)
     for copy in fields + conds_lon:
         copy.wait_send()
     sums_q = applied(l0.q, ag, lambda rows, b, v, av: (b * v, v * av), 2)
 
-    for copy in fields_lon:
+    for copy in fields:
         copy.wait_recv()
 
     def first(r):
@@ -444,10 +448,8 @@
     for i, x in enumerate(seven):
         total = jnp.where(row == i, jnp.sum(x, axis=0, keepdims=True), total)
     t1[...] = total
-    for d in range(1, 16):
+    for d in FAR1:
         send(t1, got1.at[d - 1], c1_send, c1_recv, 0, mate1(d))
-    for copy in fields_lon:
-        copy.wait_send()
     wait_all(got1, c1_recv)
 
     def gathered(total, got):
@@ -458,7 +460,7 @@
 
     total = gathered(total, got1)
     t2[...] = total
-    for d in range(1, 16):
+    for d in FAR2:
         send(t2, got2.at[d - 1], c2_send, c2_recv, 0, mate2(d))
     wait_all(got1, c1_send)
     wait_all(got2, c2_recv)
@@ -490,7 +492,7 @@
     scratch += [vm(3, 5, 64 + 2 * PAD2, 128), vm(8, 128), vm(15, 8, 128), vm(8, 128), vm(15, 8, 128)]
     scratch += wide(N0 + 2 * PAD, 9) + wide(N0 // 2 + 2 * PAD, 13) + wide(64 + 2 * PAD2, 10)
     scratch += wide(32 + 2 * PAD, 13) + wide(16 + 2 * PAD, 13) + wide(8 + 2 * PAD, 14)
-    scratch += [dma((3, 4)), dma((8,)), dma((8,)), dma((7,)), dma((7,)), dma((7,)), dma((7,))] + [dma((1,))] * 4
+    scratch += [dma((3, 4)), dma((8,)), dma((8,)), dma((7,)), dma((7,)), dma((19,)), dma((19,))] + [dma((1,))] * 4
     return pl.pallas_call(
         kernel,
         out_shape=(jax.ShapeDtypeStruct((ROWS, COLS), F32),) * 2,

time: 43.4 us -> 40.6 us (0.935)
  Pallas kernels: 40.3 us -> 37.5 us
    pallas_call x1, Pallas kernels: 40.3 us -> 37.5 us  [body(): pl.pallas_call(kernel, out_shape=(jax.ShapeDtypeStruct((ROWS, COLS), F32)...]
where the time goes in v3:
time: 40.6 us; the launch traced here: 40.4 us
  Pallas kernels  37.5 us (92%)
  local copies, waits for them, and re-layouts  2.26 us (6%)
  between operations  0.65 us (2%)
    pallas_call x1, Pallas kernels, body(): pl.pallas_call(kernel, out_shape=(jax.ShapeDtypeStruct((ROWS, COLS), F32)...  37.5 us
    unnamed x4, local copies, waits for them, and re-layouts  2.26 us

profile of v3, /device:TPU:1, one launch (start us, length us, event | category | flops | bytes accessed | tf_op | source)
XLA Modules:
  0.0 40.4 jit_solution(5363486456354505935)
XLA Ops:
  0.6 37.5 %shard_map.50 = (f32[64,512]{1,0:T(8,128)}, f32[64,512]{1,0:T(8,128)}) custom-call(f32[64,512]{1,0:T(8,128)} %b_in.1, f32[64,512]{1,0:T(8,128)} %e_in.1, f32[64,512]{1,0:T(8,128)} %s_in.1), custom_call_target="tpu_custom_call" | custom-call | flops 10000000 | bytes 655360 | tf_op jit(solution)/shard_map/pallas_call | solution.py:496
  38.1 0.0 copy-start
  38.1 1.6 %copy.7 = f32[64,512]{1,0:T(8,128)} copy(f32[64,512]{1,0:T(8,128)} %get-tuple-element.4) | data formatting | bytes 262144
  39.7 0.0 copy-done
  39.8 0.7 %copy.8 = f32[64,512]{1,0:T(8,128)} copy(f32[64,512]{1,0:T(8,128)S(1)} %copy-done) | data formatting | bytes 262144
Async XLA Ops:
  38.1 1.6 %copy-start = (f32[64,512]{1,0:T(8,128)S(1)}, f32[64,512]{1,0:T(8,128)}, u32[]{:S(2)}) copy-start(f32[64,512]{1,0:T(8,128)} %get-tuple-element.5) | copy-start | bytes 393220

commit v4 on v3

--- a/solution.py
+++ b/solution.py
@@ -253,17 +253,6 @@
 
     own_rows = pl.ds(pl.multiple_of(PAD2 + lat * 16, 16), 16)
 
-    for a in range(0, 16, 8):
-        x = ld(g.at[1], top + 4 * a, 8, range(4), 4)
-        for j in (1, 2, 3):
-            x = x + ld(g.at[1], top + 4 * a + j, 8, range(4), 4)
-        y = ld(g.at[2], top + 4 * a + 3, 8, range(4), 4)
-        y = y + roll_l(y, -1)
-        y = y + roll_l(y, -2)
-        rows = pl.ds(pl.multiple_of(PAD2 + lat * 16 + a, 8), 8)
-        c[1, 2, rows, :] = compact(x, 3)
-        c[2, 2, rows, :] = compact(y, 0)
-
     pl.semaphore_wait(barrier, len(greeted))
 
     def send(src, dst, s_sem, r_sem, k, to):
@@ -296,13 +285,21 @@
             for k, d in enumerate(SPREAD_LON)
         ]
 
+    for a in range(0, 16, 8):
+        x = ld(g.at[1], top + 4 * a, 8, range(4), 4)
+        for j in (1, 2, 3):
+            x = x + ld(g.at[1], top + 4 * a + j, 8, range(4), 4)
+        y = ld(g.at[2], top + 4 * a + 3, 8, range(4), 4)
+        y = y + roll_l(y, -1)
+        y = y + roll_l(y, -2)
+        rows = pl.ds(pl.multiple_of(PAD2 + lat * 16 + a, 8), 8)
+        c[1, 2, rows, :] = compact(x, 3)
+        c[2, 2, rows, :] = compact(y, 0)
+
     conds = spread_lat(pl.ds(1, 2), cs_send, cs_recv)
 
     for copy in halos:
         copy.wait_recv()
-    for copy in conds:
-        copy.wait_recv()
-    conds_lon = spread_lon(pl.ds(1, 2), cs_send, cs_recv)
 
     has_north = jnp.where(lat > 0, 1.0, 0.0).astype(F32)
     used = (l8 < 16) | (l8 >= 112)
@@ -318,6 +315,9 @@
 
     coeffs(l0, 16, bounds(H, ROWS), True)
     sweep(l0, l0.wf, l0.v, True, 0, N0, 16)
+    for copy in conds:
+        copy.wait_recv()
+    conds_lon = spread_lon(pl.ds(1, 2), cs_send, cs_recv)
     coarsen(l0, l1)
     remainder(l0, 16)
     coeffs(l1, 16, bounds(H // 2, ROWS // 2))
@@ -495,12 +495,12 @@
     scratch += [dma((3, 4)), dma((8,)), dma((8,)), dma((7,)), dma((7,)), dma((19,)), dma((19,))] + [dma((1,))] * 4
     return pl.pallas_call(
         kernel,
-        out_shape=(jax.ShapeDtypeStruct((ROWS, COLS), F32),) * 2,
+        out_shape=(pltpu.VMEM((ROWS, COLS), F32),) * 2,
         in_specs=[pl.BlockSpec(memory_space=pltpu.HBM)] * 3,
         out_specs=(pl.BlockSpec(memory_space=pltpu.VMEM),) * 2,
         scratch_shapes=scratch,
         compiler_params=pltpu.CompilerParams(
-            collective_id=0, has_side_effects=True, vmem_limit_bytes=63 * 1024 * 1024
+            collective_id=0, has_side_effects=True, vmem_limit_bytes=60 * 1024 * 1024
         ),
         cost_estimate=pl.CostEstimate(flops=10_000_000, bytes_accessed=655360, transcendentals=0),
     )(guidance, cond_lon, cond_lat)

time: 40.6 us -> 38.9 us (0.958)
  local copies, waits for them, and re-layouts: 2.26 us -> 1.31 us
  Pallas kernels: 37.5 us -> 36.8 us
    unnamed x4 -> x2, local copies, waits for them, and re-layouts: 2.26 us -> 1.31 us
    pallas_call x1, Pallas kernels: 37.5 us -> 36.8 us  [body(): pl.pallas_call(kernel, out_shape=(pltpu.VMEM((ROWS, COLS), F32),) * 2, in...]
where the time goes in v4:
time: 38.9 us; the launch traced here: 38.8 us
  Pallas kernels  36.8 us (95%)
  local copies, waits for them, and re-layouts  1.31 us (3%)
  between operations  0.64 us (2%)
    pallas_call x1, Pallas kernels, body(): pl.pallas_call(kernel, out_shape=(pltpu.VMEM((ROWS, COLS), F32),) * 2, in...  36.8 us
    unnamed x2, local copies, waits for them, and re-layouts  1.31 us

profile of v4, /device:TPU:1, one launch (start us, length us, event | category | flops | bytes accessed | tf_op | source)
XLA Modules:
  0.0 38.8 jit_solution(13761848878343649111)
XLA Ops:
  0.6 36.8 %shard_map.50 = (f32[64,512]{1,0:T(8,128)S(1)}, f32[64,512]{1,0:T(8,128)S(1)}) custom-call(f32[64,512]{1,0:T(8,128)} %b_in.1, f32[64,512]{1,0:T(8,128)} %e_in.1, f32[64,512]{1,0:T(8,128)} %s_in.1), custom_call_target="tpu_custom_call" | custom-call | flops 10000000 | bytes 655360 | tf_op jit(solution)/shard_map/pallas_call | solution.py:496
  37.5 0.7 %copy.7 = f32[64,512]{1,0:T(8,128)} copy(f32[64,512]{1,0:T(8,128)S(1)} %get-tuple-element.2) | data formatting | bytes 262144
  38.1 0.7 %copy.8 = f32[64,512]{1,0:T(8,128)} copy(f32[64,512]{1,0:T(8,128)S(1)} %get-tuple-element.3) | data formatting | bytes 262144
